TPU v7x, 128 devices: a whole 4x4x4 slice. The times are simulated.
128 devices in a mesh: member: 4 (over x), group: 32 (over y, z, core).
Axes of the slice: x: 4, y: 4, z: 4, core: 2. Of those that a mesh axis runs over, the one named last changes fastest.
Arguments:
- agg_one: bfloat16 [65536, 768], P(('member', 'group')), may hold values from -6 to 6
- agg_two: bfloat16 [65536, 768], P(('member', 'group')), may hold values from -6 to 6
- grad_out: bfloat16 [65536, 768], P(('member', 'group')), may hold values from -6 to 6
- hop_one_weight: bfloat16 [768, 768], replicated, may hold values from -0.21875 to 0.21875
- hop_two_weight: bfloat16 [768, 768], replicated, may hold values from -0.21875 to 0.21875
- block_values: bfloat16 [6144, 256, 256], P(('member', 'group')), may hold values from 0 to 0.046875
- src_slot: int32 [128, 48], P(('member', 'group')), may hold values from 0 to 37, as said below
- dst_block: int32 [128, 48], P(('member', 'group')), may hold values from 0 to 1
- block_count: int32 [128], P(('member', 'group')), may hold values from 33 to 48, as said below
- send_member: int32 [128, 4, 1], P(('member', 'group')), may hold values from 0 to 1, as said below
- send_group: int32 [128, 32], P(('member', 'group')), may hold values from 0 to 1, as said below
Outputs:
- grad_emb: bfloat16 [65536, 768], P(('member', 'group'))
- grad_w_one: float32 [768, 768], replicated
- grad_w_two: float32 [768, 768], replicated
Inputs may be any that keep to these rules, and one draw needn't show every extreme that they name: `send_member`: for device d, entry [d, p, 0] is the label block of d, counted within d, sent to the device of member index p in d's group; one for every p. `send_group`: entry [d, h] is the label block of d, counted within d, sent to the device of group h with d's member index; one for every h. The first block_count[d] slots of device d are live, the rest hold 0 in src_slot and dst_block and are not read; some device has all 48 slots live. `src_slot`: For device d of group g, slot j < 32 - 1 holds 2 + 4 + ((g + 1 + j) % 32); every later slot holds a value under 2 + 4.
All inputs are finite; a program needn't handle non-finite values.
Results may differ from a plain program's by a relative error of at most 0.0065.
Values may be sent and summed in bfloat16 or wider, within the bound.
A program may use at most 128 MiB of HBM per device.

v0:
```python
import jax
import jax.numpy as jnp
from jax import lax
from jax.sharding import PartitionSpec as P


def silu_slope(value):
    sig = jax.nn.sigmoid(value)
    return sig * (1.0 + value * (1.0 - sig))


def slot_sweep(pool, pool_index, block_values, targets, live_count, first_base, local_blocks):
    slot_total = block_values.shape[0]
    block_ids = jnp.arange(local_blocks, dtype=jnp.int32)
    loop_turns = (live_count - first_base + 3) // 4

    def block_step(turn, summed):
        slot_pos = first_base + turn * 4 + jnp.arange(4, dtype=jnp.int32)
        live_mask = slot_pos < live_count
        clipped = jnp.minimum(slot_pos, slot_total - 1)
        pool_pick = jnp.clip(pool_index[clipped], 0, pool.shape[0] - 1)
        block_vals = block_values[clipped]
        target_col = targets[clipped]
        pieces = pool[pool_pick]
        products = jnp.einsum(
            "kab,kad->kbd", block_vals, pieces, preferred_element_type=jnp.float32
        )
        one_hot = ((target_col[:, None] == block_ids[None, :]) & live_mask[:, None]).astype(
            jnp.float32
        )
        return summed + jnp.einsum("kr,kbd->rbd", one_hot, products)

    start_sum = jnp.zeros((local_blocks, pool.shape[1], pool.shape[2]), jnp.float32)
    return lax.fori_loop(0, loop_turns, block_step, start_sum)


def transposed_aggregate(
    field, block_values, src_slot, dst_block, block_count, send_member, send_group
):
    block_rows = block_values.shape[1]
    feature_width = field.shape[1]
    local_blocks = field.shape[0] // block_rows
    members = lax.axis_size("member")
    groups = lax.axis_size("group")
    capacity = send_member.shape[2]
    blocks = field.reshape(local_blocks, block_rows, feature_width)
    slot_ids = src_slot[0]
    member_off = slot_ids - local_blocks
    cross_off = member_off - members * capacity
    targets = dst_block[0]
    live_count = block_count[0]
    gathered, lists = (
        lax.all_gather(field, "member", axis=0, tiled=True),
        lax.all_gather(send_member[0], "member", axis=0, tiled=True),
    )
    own_member = lax.axis_index("member")
    clipped = jnp.clip(member_off, 0, members * capacity - 1)
    peer_member = clipped // capacity
    which_slot = clipped % capacity
    chosen = lists[peer_member * members + own_member, which_slot]
    member_index = peer_member * local_blocks + chosen
    member_pool = gathered.reshape(members * local_blocks, block_rows, feature_width)
    member_total = members * local_blocks
    cross_out = blocks[send_group[0]]
    pool_index = jnp.where(
        member_off < 0,
        slot_ids,
        jnp.where(
            cross_off < 0, local_blocks + member_index, local_blocks + member_total + cross_off
        ),
    ).astype(jnp.int32)
    cross_in = lax.all_to_all(
        cross_out.reshape(groups * block_rows, feature_width),
        "group",
        split_axis=0,
        concat_axis=0,
        tiled=True,
    ).reshape(groups, block_rows, feature_width)
    pool = jnp.concatenate([blocks, member_pool, cross_in], 0)
    summed = slot_sweep(pool, pool_index, block_values, targets, live_count, 0, local_blocks)
    return summed.reshape(field.shape[0], feature_width)


def weight_total(partial_value):
    return lax.psum(partial_value, ("member", "group"))


def weight_part(aggregate, pulled):
    return lax.dot_general(
        aggregate, pulled, (((0,), (0,)), ((), ())), preferred_element_type=jnp.float32
    )


def times_transpose(left, weight):
    return lax.dot_general(
        left, weight, (((1,), (1,)), ((), ())), preferred_element_type=jnp.float32
    )


def body(
    agg_one,
    agg_two,
    grad_out,
    hop_one_weight,
    hop_two_weight,
    block_values,
    src_slot,
    dst_block,
    block_count,
    send_member,
    send_group,
):
    total_labels = agg_one.shape[0] * lax.axis_size("member") * lax.axis_size("group")
    grad_scale = float(total_labels) ** (-0.5)
    graph = (block_values, src_slot, dst_block, block_count, send_member, send_group)
    lift_one = jnp.dot(agg_one, hop_one_weight, preferred_element_type=jnp.float32)
    lift_two = jnp.dot(agg_two, hop_two_weight, preferred_element_type=jnp.float32)
    pull_two = (grad_out.astype(jnp.float32) * silu_slope(lift_two)).astype(jnp.bfloat16)
    part_two = weight_part(agg_two, pull_two)
    grad_w_two = weight_total(part_two) * grad_scale
    back_two = times_transpose(pull_two, hop_two_weight).astype(jnp.bfloat16)
    carry_grad = grad_out.astype(jnp.float32) + transposed_aggregate(back_two, *graph)
    pull_one = (carry_grad * silu_slope(lift_one)).astype(jnp.bfloat16)
    part_one = weight_part(agg_one, pull_one)
    grad_w_one = weight_total(part_one) * grad_scale
    back_one = times_transpose(pull_one, hop_one_weight).astype(jnp.bfloat16)
    grad_emb = (carry_grad + transposed_aggregate(back_one, *graph)).astype(jnp.bfloat16)
    return (grad_emb, grad_w_one, grad_w_two)


def solution(mesh):
    in_specs = (
        P(("member", "group"), None),
        P(("member", "group"), None),
        P(("member", "group"), None),
        P(),
        P(),
        P(("member", "group"), None, None),
        P(("member", "group"), None),
        P(("member", "group"), None),
        P(("member", "group")),
        P(("member", "group"), None, None),
        P(("member", "group"), None),
    )
    out_specs = (P(("member", "group"), None), P(), P())
    return jax.shard_map(body, mesh=mesh, in_specs=in_specs, out_specs=out_specs, check_vma=False)
```

profile of v0, /device:TPU:1, one launch (start us, length us, event | category | flops | bytes accessed | tf_op | source)
XLA Modules:
  0.0 1038.6 jit_solution(9030329349742898792)
XLA Ops:
  11.8 6.6 gather_fusion.9
  18.4 9.7 all-to-all-start
  30.9 7.5 all-reduce.1
  39.3 32.3 %all-gather.4.cloned.1.call-done = bf16[2048,768]{1,0:T(8,128)(2,1)} async-done(((bf16[512,768]{1,0:T(8,128)(2,1)}), bf16[2048,768]{1,0:T(8,128)(2,1)}) %all-gather.4.cloned.1.call-update) | async-done | bytes 3145744 | tf_op jit(solution)/shard_map/all_gather | solution.py:53
  71.6 131.1 %all-to-all-done = bf16[32,256,768]{2,1,0:T(8,128)(2,1)} async-done(((bf16[32,256,768]{2,1,0:T(8,128)(2,1)}), bf16[32,256,768]{2,1,0:T(8,128)(2,1)}, u32[]{:S(2)}, u32[]{:S(2)}) %all-to-all-start) | async-done | bytes 12582944 | tf_op jit(solution)/shard_map/all_to_all | solution.py:72
  202.8 13.3 %pad_maximum_fusion = bf16[42,256,768]{2,1,0:T(8,128)(2,1)} fusion(bf16[32,256,768]{2,1,0:T(8,128)(2,1)} %all-to-all-done, bf16[8,256,768]{2,1,0:T(8,128)(2,1)} %bitcast.116, bf16[2,256,768]{2,1,0:T(8,128)(2,1)S(1)} %bitcast.113), kind=kLoop, calls=%fused_computation.45 | loop fusion | flops 16515072 | bytes 33030144 | tf_op jit(solution)/shard_map/concatenate | solution.py:79
  217.6 217.0 %while.22 = (s32[]{:T(128)}, f32[2,256,768]{2,0,1:T(2,128)}, s32[]{:T(128)}, s32[48]{0:T(128)S(1)}, s32[]{:T(128)}, /*index=5*/bf16[48,256,256]{2,1,0:T(8,128)(2...) while((s32[]{:T(128)}, f32[2,256,768]{2,0,1:T(2,128)}, s32[]{:T(128)}, ...), condition=%wide.region_1.2_spmd.clone, body=%wide.region_0.0_spmd.clone.sunk | while | flops 406194240 | bytes 12591469 | solution.py:34
  221.7 6.3 gather_fusion.2
  231.1 4.6 fusion.80
  239.8 6.3 gather_fusion.2
  249.2 4.6 fusion.80
  257.9 6.3 gather_fusion.2
  267.3 4.6 fusion.80
  275.9 6.3 gather_fusion.2
  285.4 4.6 fusion.80
  294.0 6.3 gather_fusion.2
  303.4 4.6 fusion.80
  312.1 6.3 gather_fusion.2
  321.5 4.6 fusion.80
  330.2 6.3 gather_fusion.2
  339.6 4.6 fusion.80
  348.3 6.3 gather_fusion.2
  357.7 4.6 fusion.80
  366.4 6.3 gather_fusion.2
  375.8 4.6 fusion.80
  384.4 6.3 gather_fusion.2
  402.5 6.3 gather_fusion.2
  412.0 4.6 fusion.80
  420.6 6.3 gather_fusion.2
  430.0 4.6 fusion.80
  438.9 6.7 gather_fusion.10
  445.6 23.2 %all-to-all-start.1 = ((bf16[32,256,768]{2,1,0:T(8,128)(2,1)}), bf16[32,256,768]{2,1,0:T(8,128)(2,1)}, u32[]{:S(2)}, u32[]{:S(2)}) async-start(bf16[32,256,768]{2,1,0:T(8,128)(2,1)} %gather_fusion.10), calls=%async_computation.1 | async-start | bytes 25165824 | tf_op jit(solution)/shard_map/all_to_all | solution.py:72
  474.1 282.5 %all-reduce.5.cloned.1.call-done = (f32[768,768]{0,1:T(8,128)}, f32[768,768]{0,1:T(8,128)}) async-done(((f32[768,768]{0,1:T(8,128)}, f32[768,768]{0,1:T(8,128)}), (f32[768,768]{0,1:T(8,128)}, f32[768,768]{0,1:T(8,128)})) %all-reduce.5.cloned.1.call-update) | async-done | bytes 4718608 | tf_op jit(solution)/shard_map/psum | solution.py:85
  765.7 31.1 %all-gather.6.cloned.1.call-done = bf16[2048,768]{1,0:T(8,128)(2,1)} async-done(((bf16[512,768]{1,0:T(8,128)(2,1)}), bf16[2048,768]{1,0:T(8,128)(2,1)}) %all-gather.6.cloned.1.call-update) | async-done | bytes 3145744 | tf_op jit(solution)/shard_map/all_gather | solution.py:53
  796.8 13.3 %pad_maximum_fusion.1 = bf16[42,256,768]{2,1,0:T(8,128)(2,1)} fusion(bf16[32,256,768]{2,1,0:T(8,128)(2,1)} %all-to-all-done.1, bf16[8,256,768]{2,1,0:T(8,128)(2,1)} %bitcast.117, bf16[2,256,768]{2,1,0:T(8,128)(2,1)S(1)} %bitcast.115), kind=kLoop, calls=%fused_computation.46 | loop fusion | flops 16515072 | bytes 33030144 | tf_op jit(solution)/shard_map/concatenate | solution.py:79
  811.7 217.2 %while.23 = (s32[]{:T(128)}, f32[2,256,768]{2,0,1:T(2,128)}, s32[]{:T(128)}, s32[48]{0:T(128)S(1)}, s32[]{:T(128)}, /*index=5*/bf16[48,256,256]{2,1,0:T(8,128)(2...) while((s32[]{:T(128)}, f32[2,256,768]{2,0,1:T(2,128)}, s32[]{:T(128)}, ...), condition=%wide.region_3.4_spmd.clone, body=%wide.region_2.3_spmd.clone.sunk | while | flops 406194240 | bytes 12591469 | solution.py:34
  815.7 6.3 gather_fusion.6
  833.8 6.3 gather_fusion.6
  851.9 6.3 gather_fusion.6
  870.0 6.3 gather_fusion.6
  888.1 6.3 gather_fusion.6
  906.2 6.3 gather_fusion.6
  924.3 6.3 gather_fusion.6
  942.4 6.3 gather_fusion.6
  960.5 6.3 gather_fusion.6
  978.6 6.3 gather_fusion.6
  996.7 6.3 gather_fusion.6
  1014.8 6.3 gather_fusion.6
  (296 shorter events, 262.1 us)
Async XLA Ops:
  7.2 1.3 copy-start
  10.9 0.8 copy-start.15
  11.7 6.7 copy-start.3
  18.4 11.2 %copy-start.18 = (u32[128]{0:T(128)S(1)}, u32[128]{0:T(128)}, u32[]{:S(2)}) copy-start(u32[128]{0:T(128)} %constant.133) | copy-start | bytes 1540
  18.4 12.4 %copy-start.16 = (s32[1,4,1]{1,2,0:T(1,128)S(1)}, s32[1,4,1]{1,2,0:T(1,128)}, u32[]{:S(2)}) copy-start(s32[1,4,1]{1,2,0:T(1,128)} %param.24) | copy-start | bytes 52
  18.4 20.1 %copy-start.17 = (s32[1,48]{1,0:T(1,128)S(1)}, s32[1,48]{1,0:T(1,128)}, u32[]{:S(2)}) copy-start(s32[1,48]{1,0:T(1,128)} %param.21) | copy-start | bytes 580
  18.4 184.4 %all-to-all-start = ((bf16[32,256,768]{2,1,0:T(8,128)(2,1)}), bf16[32,256,768]{2,1,0:T(8,128)(2,1)}, u32[]{:S(2)}, u32[]{:S(2)}) async-start(bf16[32,256,768]{2,1,0:T(8,128)(2,1)} %gather_fusion.9), calls=%async_computation | async-start | bytes 25165824 | tf_op jit(solution)/shard_map/all_to_all | solution.py:72
  28.1 174.7 %copy-start.4 = (bf16[512,768]{1,0:T(8,128)(2,1)S(1)}, bf16[512,768]{1,0:T(8,128)(2,1)}, u32[]{:S(2)}) copy-start(bf16[512,768]{1,0:T(8,128)(2,1)} %copy-done.3) | copy-start | bytes 2359300
  28.1 43.5 %all-gather.4.cloned.1.call-start = ((), (), s32[]{:S(2)}) async-start(), calls=%async_computation.2 | async-start | bytes 3932160 | tf_op jit(solution)/shard_map/all_gather | solution.py:53
  216.1 1.6 copy-start.2
  434.7 1.7 copy-start.9
  434.7 1.8 copy-start.12
  434.7 2.2 copy-start.14
  436.9 1.2 copy-start.7
  438.9 6.7 copy-start.5
  445.6 23.3 %copy-start.11 = (bf16[512,768]{1,0:T(8,128)(2,1)S(1)}, bf16[512,768]{1,0:T(8,128)(2,1)}, u32[]{:S(2)}) copy-start(bf16[512,768]{1,0:T(8,128)(2,1)} %param.16) | copy-start | bytes 2359300
  445.6 351.2 %all-to-all-start.1 = ((bf16[32,256,768]{2,1,0:T(8,128)(2,1)}), bf16[32,256,768]{2,1,0:T(8,128)(2,1)}, u32[]{:S(2)}, u32[]{:S(2)}) async-start(bf16[32,256,768]{2,1,0:T(8,128)(2,1)} %gather_fusion.10), calls=%async_computation.1 | async-start | bytes 25165824 | tf_op jit(solution)/shard_map/all_to_all | solution.py:72
  468.8 2.3 copy-start.13
  468.8 287.8 %all-reduce.5.cloned.1.call-start = ((), (), s32[]{:S(2)}) async-start(), calls=%async_computation.4 | async-start | bytes 9437184 | tf_op jit(solution)/shard_map/psum | solution.py:85
  473.4 323.5 %all-gather.6.cloned.1.call-start = ((), (), s32[]{:S(2)}) async-start(), calls=%async_computation.3 | async-start | bytes 3932160 | tf_op jit(solution)/shard_map/all_gather | solution.py:53
  763.8 33.1 %copy-start.6 = (bf16[512,768]{1,0:T(8,128)(2,1)S(1)}, bf16[512,768]{1,0:T(8,128)(2,1)}, u32[]{:S(2)}) copy-start(bf16[512,768]{1,0:T(8,128)(2,1)} %copy-done.5) | copy-start | bytes 2359300
  1028.8 1.9 copy-start.8
  1028.8 2.1 copy-start.10
  1028.8 3.2 copy-start.1
Sparse Core Ops, SparseCore 0:
  31.2 40.3 all-gather.3
  475.3 281.3 all-reduce.4
  758.9 37.9 all-gather.5
where the time goes:
time: 1040 us
  waiting for transfers between devices  478 us (46%)
  local copies, waits for them, and re-layouts  292 us (28%)
  matrix products  163 us (16%)
  other arithmetic  48.2 us (5%)
  starting transfers between devices  33.2 us (3%)
  between operations  15.3 us (1%)
    psum x1, waiting for transfers between devices, weight_total(): return lax.psum(partial_value, ('member', 'group'))  283 us
    gather x24, local copies, waits for them, and re-layouts, block_step(): pieces = pool[pool_pick]  152 us
    all_to_all x2, waiting for transfers between devices, transposed_aggregate(): lax.all_to_all(cross_out.reshape(groups * block_rows, feature_width), 'gr...  131 us
    dot_general x24, matrix products, block_step(): return summed + jnp.einsum('kr,kbd->rbd', one_hot, products)  111 us
    gather x24, local copies, waits for them, and re-layouts, block_step(): block_vals = block_values[clipped]  80.7 us
    all_gather x2, waiting for transfers between devices, transposed_aggregate(): lax.all_gather(field, 'member', axis=0, tiled=True)  63.4 us
    dot_general x24, matrix products, block_step(): jnp.einsum('kab,kad->kbd', block_vals, pieces, preferred_element_type=jnp...  42.7 us
    all_to_all x2, starting transfers between devices, transposed_aggregate(): lax.all_to_all(cross_out.reshape(groups * block_rows, feature_width), 'gr...  32.9 us
  transfers between devices with their start and end apart: 5, of which 4 were waited for; matrix products, arithmetic and copies ran while one was open for 1% of the time, Pallas kernels for 0%

commit v1 on v0

v1 whole, which is shorter than its diff:
```python
import functools

import jax
import jax.numpy as jnp
from jax import lax
from jax.experimental import pallas as pl
from jax.experimental.pallas import tpu as pltpu
from jax.sharding import PartitionSpec as P

MESH = pl.DeviceIdType.MESH
SIDE = 4

ARRIVE = (
    (((1, 0, 0), (3, 0, 0), (0, 1, 1), (0, 3, 1)), ()),
    (((1, 0, 1), (3, 0, 1), (0, 1, 0), (0, 3, 0)), ((1, 0), (3, 0), (0, 1), (0, 3))),
    (((2, 0, 0), (0, 2, 1)), ()),
    (((1, 1, 1), (3, 1, 1), (1, 1, 0), (1, 3, 0)), ((1, 1),)),
    (((1, 3, 1), (3, 3, 1), (3, 1, 0), (3, 3, 0)), ((1, 3), (3, 1), (3, 3))),
    (((2, 0, 1), (0, 2, 0)), ((2, 0), (0, 2))),
    (((1, 2, 1), (3, 2, 1), (2, 1, 0), (2, 3, 0)), ()),
    (((2, 1, 1), (1, 2, 0)), ((2, 1), (1, 2))),
    (((2, 3, 1), (3, 2, 0)), ((2, 3), (3, 2))),
    (((2, 2, 1), (2, 2, 0)), ((2, 2),)),
)


def slope(value):
    sig = jax.nn.sigmoid(value)
    return sig * (1.0 + value * (1.0 - sig))


def across(left, right, dims):
    return lax.dot_general(left, right, (dims, ((), ())), preferred_element_type=jnp.float32)


def hop_kernel(
    scale,
    picks, slots, targets, count, lists,
    agg, weight, grad, values_hbm,
    out, gout,
    pool, values, member_out, member_in, pull,
    part, part_core, part_x_out, part_x_in, part_y, part_y_in, part_z, total_y, total,
    values_sem, ring_send, ring_recv, core_send, core_recv, member_send, member_recv,
    pc_send, pc_recv, px_send, px_recv, py_send, py_recv, pz_send, pz_recv,
    ty_send, ty_recv, tx_send, tx_recv, tc_send, tc_recv,
):
    blk = values.shape[1]
    width = weight.shape[0]
    slot_total = values.shape[0]
    half = blk // 2
    m = lax.axis_index("member")
    g = lax.axis_index("group")
    y, z, c = g // (2 * SIDE), (g // 2) % SIDE, g % 2

    def at(dy, dz, other=0):
        core = c if other == 0 else 1 - c
        return (((y + dy) % SIDE) * SIDE + (z + dz) % SIDE) * 2 + core

    partner = {"group": at(0, 0, 1)}

    load_values = pltpu.make_async_copy(values_hbm, values, values_sem)
    load_values.start()

    barrier = pltpu.get_barrier_semaphore()
    for d in range(1, SIDE):
        for peer in ({"group": at(d, 0)}, {"group": at(0, d)}, {"member": (m + d) % SIDE}):
            pl.semaphore_signal(barrier, inc=1, device_id=peer, device_id_type=MESH)
    pl.semaphore_signal(barrier, inc=1, device_id=partner, device_id_type=MESH)
    pl.semaphore_wait(barrier, 3 * (SIDE - 1) + 1)

    def remote(src, dst, send, recv, peer):
        return pltpu.make_async_remote_copy(
            src_ref=src, dst_ref=dst, send_sem=send, recv_sem=recv, device_id=peer, device_id_type=MESH
        )

    def ring(dy, dz, b, axis, way):
        d = dy if axis == 0 else dz
        rows = pl.ds(0, blk) if d != 2 else pl.ds(0 if way == 1 else half, half)
        sdy, sdz = ((dy - way) % SIDE, dz) if axis == 0 else (dy, (dz - way) % SIDE)
        peer = {"group": at(way, 0) if axis == 0 else at(0, way)}
        part_of = 0 if way == 1 else 1
        return remote(
            pool.at[0, sdy * SIDE + sdz, b, rows],
            pool.at[0, dy * SIDE + dz, b, rows],
            ring_send.at[dy * SIDE + dz, b, part_of],
            ring_recv.at[dy * SIDE + dz, b, part_of],
            peer,
        )

    def arrivals(dy, dz, b):
        axis, d = (1, dz) if b == 0 else (0, dy)
        if d == 0:
            axis, d = (0, dy) if b == 0 else (1, dz)
        ways = {1: (1,), 3: (-1,), 2: (1, -1)}[d]
        return [(dy, dz, b, axis, way) for way in ways]

    def to_core(r, b):
        return remote(
            pool.at[0, r, b], pool.at[1, r, b], core_send.at[r, b], core_recv.at[r, b], partner
        )

    sent = []

    def forward(dy, dz, b):
        first, second = (0, 1) if b == 0 else (1, 0)
        pos = (dy, dz)
        moved = []
        d1, d2 = pos[first], pos[second]

        def step(axis, way):
            new = list(pos)
            new[axis] = (new[axis] + way) % SIDE
            return (new[0], new[1], b, axis, way)

        if d2 == 0:
            if d1 == 0:
                moved += [step(first, 1), step(first, -1)]
            elif d1 == 1:
                moved.append(step(first, 1))
            elif d1 == 3:
                moved.append(step(first, -1))
            moved += [step(second, 1), step(second, -1)]
        elif d2 == 1:
            moved.append(step(second, 1))
        elif d2 == 3:
            moved.append(step(second, -1))
        for key in moved:
            copy = ring(*key)
            copy.start()
            sent.append(copy)
        copy = to_core(dy * SIDE + dz, b)
        copy.start()
        sent.append(copy)

    rows_at = min(128, blk)

    for b in range(2):

        @pl.loop(0, blk // rows_at)
        def _(i, b=b):
            inner = pl.ds(pl.multiple_of(i * rows_at, rows_at), rows_at)
            rows = pl.ds(pl.multiple_of(b * blk + i * rows_at, rows_at), rows_at)
            lift = across(agg[rows, :], weight[...], ((1,), (0,)))
            pulled = (grad[rows, :].astype(jnp.float32) * slope(lift)).astype(jnp.bfloat16)
            pull[rows, :] = pulled
            back = across(pulled, weight[...], ((1,), (1,))).astype(jnp.bfloat16)
            pool[0, 0, b, inner, :] = back

        forward(0, 0, b)

    cut = min(256, width)

    @pl.loop(0, width // cut)
    def _(i):
        rows = pl.ds(pl.multiple_of(i * cut, cut), cut)
        part[rows, :] = across(agg[:, rows], pull[...], ((0,), (0,))) * scale

    half_rows, x_rows = width // 2, width // 8
    y_rows = x_rows // SIDE
    mine = pl.ds(pl.multiple_of(c * half_rows, half_rows), half_rows)
    theirs = pl.ds(pl.multiple_of((1 - c) * half_rows, half_rows), half_rows)
    pc = remote(part.at[theirs], part_core, pc_send, pc_recv, partner)
    pc.start()
    sent.append(pc)

    member_copies = []
    for d in range(1, SIDE):
        chosen = lists[(m + d) % SIDE]
        member_out[d - 1] = jnp.where(chosen == 0, pool[0, 0, 0], pool[0, 0, 1])
        copy = remote(
            member_out.at[d - 1], member_in.at[2 + m], member_send.at[d - 1], member_recv.at[d - 1],
            {"member": (m + d) % SIDE},
        )
        copy.start()
        sent.append(copy)
    member_in[0] = pool[0, 0, 0]
    member_in[1] = pool[0, 0, 1]
    member_in[2 + m] = jnp.where(lists[m] == 0, pool[0, 0, 0], pool[0, 0, 1])

    out[...] = grad[...].astype(jnp.float32)
    load_values.wait()

    @pl.loop(0, slot_total)
    def _(k):
        values[k] = values[k].T

    def cols_of(n):
        return pl.ds(pl.multiple_of(n * cut, cut), cut)

    def kept(k, live):
        value = values[k]
        zero = jnp.zeros_like(value)
        where = targets[k]
        return (
            jnp.where(jnp.logical_and(live, where == 0), value, zero),
            jnp.where(jnp.logical_and(live, where == 1), value, zero),
        )

    def sweep(other, sources):
        groups = 2 * SIDE * SIDE

        @pl.loop(0, width // cut)
        def _(n):
            cols = cols_of(n)
            top, low = out[0:blk, cols], out[blk:2 * blk, cols]
            for dy, dz in sources:
                source = at(-dy, -dz, other)
                k = (source - g - 1 + groups) % groups
                r = dy * SIDE + dz
                first, second = kept(k, True)
                block = jnp.where(picks[source] == 0, pool[other, r, 0, :, cols], pool[other, r, 1, :, cols])
                top += across(first, block, ((1,), (0,)))
                low += across(second, block, ((1,), (0,)))
            out[0:blk, cols] = top
            out[blk:2 * blk, cols] = low

    def take_core(r):
        for b in range(2):
            to_core(r, b).wait_recv()

    def px_copy(d):
        rows = pl.ds(pl.multiple_of(((m + d) % SIDE) * x_rows, x_rows), x_rows)
        return remote(
            part_x_out.at[rows], part_x_in.at[d - 1], px_send.at[d - 1], px_recv.at[d - 1],
            {"member": (m + d) % SIDE},
        )

    def py_copy(d):
        rows = pl.ds(pl.multiple_of(((y + d) % SIDE) * y_rows, y_rows), y_rows)
        return remote(
            part_y.at[rows], part_y_in.at[d - 1], py_send.at[d - 1], py_recv.at[d - 1],
            {"group": at(d, 0)},
        )

    def pz_copy(d):
        return remote(
            part_z.at[z], part_z.at[z], pz_send.at[d - 1], pz_recv.at[d - 1], {"group": at(0, d)}
        )

    def ty_copy(d):
        rows = pl.ds(pl.multiple_of(y * y_rows, y_rows), y_rows)
        return remote(
            total_y.at[rows], total_y.at[rows], ty_send.at[d - 1], ty_recv.at[d - 1], {"group": at(d, 0)}
        )

    def tx_copy(d):
        rows = pl.ds(pl.multiple_of(c * half_rows + m * x_rows, x_rows), x_rows)
        return remote(
            total.at[rows], total.at[rows], tx_send.at[d - 1], tx_recv.at[d - 1],
            {"member": (m + d) % SIDE},
        )

    tc = remote(total.at[mine], total.at[mine], tc_send, tc_recv, partner)

    def launch(copies):
        for copy in copies:
            copy.start()
            sent.append(copy)

    def grad_step(number):
        peers = range(1, SIDE)
        if number == 0:
            pc.wait_recv()
            part[mine, :] += part_core[...]
            part_x_out[...] = part[mine, :].astype(jnp.bfloat16)
            launch([px_copy(d) for d in peers])
        elif number == 1:
            for d in peers:
                px_copy(d).wait_recv()
            rows = pl.ds(pl.multiple_of(c * half_rows + m * x_rows, x_rows), x_rows)
            summed = part[rows, :]
            for d in peers:
                summed += part_x_in[d - 1].astype(jnp.float32)
            part_y[...] = summed
            launch([py_copy(d) for d in peers])
        elif number == 2:
            for d in peers:
                py_copy(d).wait_recv()
            rows = pl.ds(pl.multiple_of(y * y_rows, y_rows), y_rows)
            summed = part_y[rows, :]
            for d in peers:
                summed += part_y_in[d - 1]
            part_z[z] = summed
            launch([pz_copy(d) for d in peers])
        elif number == 3:
            for d in peers:
                pz_copy(d).wait_recv()
            rows = pl.ds(pl.multiple_of(y * y_rows, y_rows), y_rows)
            total_y[rows, :] = (part_z[0] + part_z[1]) + (part_z[2] + part_z[3])
            launch([ty_copy(d) for d in peers])
        elif number == 4:
            for d in peers:
                ty_copy(d).wait_recv()
            rows = pl.ds(pl.multiple_of(c * half_rows + m * x_rows, x_rows), x_rows)
            total[rows, :] = total_y[...].astype(jnp.bfloat16)
            launch([tx_copy(d) for d in peers])
        elif number == 5:
            for d in peers:
                tx_copy(d).wait_recv()
            launch([tc])
        elif number == 6:
            tc.wait_recv()
            gout[...] = total[...].astype(jnp.float32)

    grad_step(0)
    take_core(0)
    sweep(1, ((0, 0),))
    grad_at = {1: 1, 2: 2, 3: 3, 4: 4, 6: 5, 7: 6}

    for number, (blocks, complete) in enumerate(ARRIVE):
        for dy, dz, b in blocks:
            for key in arrivals(dy, dz, b):
                ring(*key).wait_recv()
            forward(dy, dz, b)
        if number in grad_at:
            grad_step(grad_at[number])
        if number == 5:
            for d in range(1, SIDE):
                remote(
                    member_out.at[d - 1], member_in.at[2 + (m - d + SIDE) % SIDE], member_send.at[d - 1],
                    member_recv.at[d - 1], {"member": (m + d) % SIDE},
                ).wait_recv()

            @pl.loop(2 * SIDE * SIDE - 1, slot_total)
            def _(k):
                first, second = kept(k, k < count[0])

                @pl.loop(0, width // cut)
                def _(n):
                    cols = cols_of(n)
                    block = member_in[slots[k], :, cols]
                    out[0:blk, cols] += across(first, block, ((1,), (0,)))
                    out[blk:2 * blk, cols] += across(second, block, ((1,), (0,)))

        if complete:
            sweep(0, complete)
            for dy, dz in complete:
                take_core(dy * SIDE + dz)
            sweep(1, complete)

    for copy in sent:
        copy.wait_send()


def hop(picks, slots, targets, count, lists, agg, weight, grad, values, scale, interpret=False):
    rows, width = agg.shape
    slot_total, blk, _ = values.shape
    bf16, f32 = jnp.bfloat16, jnp.float32
    half_rows, x_rows = width // 2, width // 8
    y_rows = x_rows // SIDE
    vmem, smem = pl.BlockSpec(memory_space=pltpu.VMEM), pl.BlockSpec(memory_space=pltpu.SMEM)
    dma = pltpu.SemaphoreType.DMA
    return pl.pallas_call(
        functools.partial(hop_kernel, scale),
        out_shape=(jax.ShapeDtypeStruct((rows, width), f32), jax.ShapeDtypeStruct((width, width), f32)),
        in_specs=[smem] * 5 + [vmem] * 3 + [pl.BlockSpec(memory_space=pl.ANY)],
        out_specs=(vmem, vmem),
        scratch_shapes=[
            pltpu.VMEM((2, SIDE * SIDE, 2, blk, width), bf16),
            pltpu.VMEM((slot_total, blk, blk), bf16),
            pltpu.VMEM((SIDE - 1, blk, width), bf16),
            pltpu.VMEM((2 + SIDE, blk, width), bf16),
            pltpu.VMEM((rows, width), bf16),
            pltpu.VMEM((width, width), f32),
            pltpu.VMEM((half_rows, width), f32),
            pltpu.VMEM((half_rows, width), bf16),
            pltpu.VMEM((SIDE - 1, x_rows, width), bf16),
            pltpu.VMEM((x_rows, width), f32),
            pltpu.VMEM((SIDE - 1, y_rows, width), f32),
            pltpu.VMEM((SIDE, y_rows, width), f32),
            pltpu.VMEM((x_rows, width), f32),
            pltpu.VMEM((width, width), bf16),
            dma(()),
            dma((SIDE * SIDE, 2, 2)), dma((SIDE * SIDE, 2, 2)),
            dma((SIDE * SIDE, 2)), dma((SIDE * SIDE, 2)),
            dma((SIDE - 1,)), dma((SIDE - 1,)),
            dma(()), dma(()),
            dma((SIDE - 1,)), dma((SIDE - 1,)),
            dma((SIDE - 1,)), dma((SIDE - 1,)),
            dma((SIDE - 1,)), dma((SIDE - 1,)),
            dma((SIDE - 1,)), dma((SIDE - 1,)),
            dma((SIDE - 1,)), dma((SIDE - 1,)),
            dma(()), dma(()),
        ],
        compiler_params=pltpu.CompilerParams(
            collective_id=0, has_side_effects=True, vmem_limit_bytes=60 << 20
        ),
        name="hop",
    )(picks, slots, targets, count, lists, agg, weight, grad, values)


def body(
    agg_one,
    agg_two,
    grad_out,
    hop_one_weight,
    hop_two_weight,
    block_values,
    src_slot,
    dst_block,
    block_count,
    send_member,
    send_group,
):
    total_labels = agg_one.shape[0] * lax.axis_size("member") * lax.axis_size("group")
    scale = float(total_labels) ** (-0.5)
    picks = lax.all_to_all(send_group[0], "group", split_axis=0, concat_axis=0, tiled=True)
    graph = (picks, src_slot[0], dst_block[0], block_count, send_member[0, :, 0])
    carry, grad_w_two = hop(
        *graph, agg_two, hop_two_weight, grad_out.astype(jnp.float32), block_values, scale
    )
    emb, grad_w_one = hop(*graph, agg_one, hop_one_weight, carry, block_values, scale)
    return (emb.astype(jnp.bfloat16), grad_w_one, grad_w_two)


def solution(mesh):
    in_specs = (
        P(("member", "group"), None),
        P(("member", "group"), None),
        P(("member", "group"), None),
        P(),
        P(),
        P(("member", "group"), None, None),
        P(("member", "group"), None),
        P(("member", "group"), None),
        P(("member", "group")),
        P(("member", "group"), None, None),
        P(("member", "group"), None),
    )
    out_specs = (P(("member", "group"), None), P(), P())
    return jax.shard_map(body, mesh=mesh, in_specs=in_specs, out_specs=out_specs, check_vma=False)
```

time: 1040 us -> 231 us (0.22)
  waiting for transfers between devices: 478 us -> 3.83 us
  local copies, waits for them, and re-layouts: 292 us -> 5.27 us
  Pallas kernels: 0 us -> 204 us
  matrix products: 163 us -> 0 us
  other arithmetic: 48.2 us -> 6.08 us
  starting transfers between devices: 33.2 us -> 9.6 us
  between operations: 15.3 us -> 1.31 us
    psum x1 -> x0, waiting for transfers between devices: 283 us -> none  [weight_total(): return lax.psum(partial_value, ('member', 'group'))]
    gather x99 -> x0, local copies, waits for them, and re-layouts: 278 us -> none  [the longest x24 152 us: block_step(): pieces = pool[pool_pick]]
    pallas_call x0 -> x2, Pallas kernels: none -> 204 us  [hop(): pl.pallas_call(functools.partial(hop_kernel, scale), out_shape=(jax.Shape...]
    dot_general x54 -> x0, matrix products: 163 us -> none  [the longest x24 111 us: block_step(): return summed + jnp.einsum('kr,kbd->rbd', one_hot, products)]
    all_to_all x2 -> x1, waiting for transfers between devices: 131 us -> 3.83 us  [body(): lax.all_to_all(send_group[0], 'group', split_axis=0, concat_axis=0, tiled...]
    all_gather x2 -> x0, waiting for transfers between devices: 63.4 us -> none  [transposed_aggregate(): lax.all_gather(field, 'member', axis=0, tiled=True)]
    concatenate x3 -> x0, other arithmetic: 26.6 us -> none  [the longest x2 26.6 us: transposed_aggregate(): pool = jnp.concatenate([blocks, member_pool, cross_in], 0)]
    all_to_all x2 -> x1, starting transfers between devices: 32.9 us -> 9.6 us  [body(): lax.all_to_all(send_group[0], 'group', split_axis=0, concat_axis=0, tiled...]
  transfers between devices with their start and end apart: 5 -> 1, of which waited for: 4 -> 1; matrix products, arithmetic and copies ran while one was open for 1% -> 1% of each run, Pallas kernels for 0% -> 0%
where the time goes in v1:
time: 231 us; the launch traced here: 230 us
  Pallas kernels  204 us (88%)
  starting transfers between devices  9.6 us (4%)
  other arithmetic  6.08 us (3%)
  local copies, waits for them, and re-layouts  5.27 us (2%)
  waiting for transfers between devices  3.83 us (2%)
    pallas_call x2, Pallas kernels, hop(): pl.pallas_call(functools.partial(hop_kernel, scale), out_shape=(jax.Shape...  204 us
    all_to_all x1, starting transfers between devices, body(): lax.all_to_all(send_group[0], 'group', split_axis=0, concat_axis=0, tiled...  9.6 us
  transfers between devices with their start and end apart: 1, of which 1 were waited for; matrix products, arithmetic and copies ran while one was open for 1% of the time, Pallas kernels for 0%

profile of v1, /device:TPU:1, one launch (start us, length us, event | category | flops | bytes accessed | tf_op | source)
XLA Modules:
  0.0 230.2 jit_solution(1083895199768247508)
XLA Ops:
  0.6 1.3 copy.15
  2.0 9.6 %all-to-all-start = ((s32[32,1,1]{2,1,0:T(1,128)}), s32[32,1,1]{2,1,0:T(1,128)S(1)}, u32[]{:S(2)}, u32[]{:S(2)}) async-start(s32[32,1,1]{2,1,0:T(1,128)} %copy.15), calls=%async_computation | async-start | bytes 32768 | tf_op jit(solution)/shard_map/all_to_all | solution.py:407
  12.2 2.4 %convert_element_type.6.grad = f32[512,768]{1,0:T(8,128)} convert(bf16[512,768]{1,0:T(8,128)(2,1)} %param.13) | non-fusion elementwise | flops 393216 | bytes 2359296 | tf_op jit(solution)/shard_map/convert_element_type | solution.py:410
  14.6 3.8 %all-to-all-done = s32[32,1,1]{2,1,0:T(1,128)S(1)} async-done(((s32[32,1,1]{2,1,0:T(1,128)}), s32[32,1,1]{2,1,0:T(1,128)S(1)}, u32[]{:S(2)}, u32[]{:S(2)}) %all-to-all-start) | async-done | bytes 160 | tf_op jit(solution)/shard_map/all_to_all | solution.py:407
  18.4 1.2 reduce.picks
  19.6 103.1 %hop.2 = (f32[512,768]{1,0:T(8,128)}, f32[768,768]{1,0:T(8,128)}) custom-call(s32[32]{0:T(128)} %reduce.picks, s32[48]{0:T(128)} %bitcast.4, s32[48]{0:T(128)} %bitcast.6, s32[1]{0:T(128)S(6)} %copy.18.count, s32[4]{0:T(128)} %bitcast.8, bf16[512,768]{1,0:T(8,128)(2,1)} %agg.2, bf16[768,768]{1,0:T(8,128)(2,1)} %weight.2, ...), custom_call_target="tpu_custom_call" | custom-call | tf_op jit(solution)/shard_map/hop/pallas_call | solution.py:353
  122.7 101.0 %hop.3 = (f32[512,768]{1,0:T(8,128)}, f32[768,768]{1,0:T(8,128)}) custom-call(s32[32]{0:T(128)} %reduce.picks, s32[48]{0:T(128)} %bitcast.5, s32[48]{0:T(128)} %bitcast.7, s32[1]{0:T(128)S(6)} %copy.18.count, s32[4]{0:T(128)} %bitcast.9, bf16[512,768]{1,0:T(8,128)(2,1)} %agg.3, bf16[768,768]{1,0:T(8,128)(2,1)} %weight.3, f32[512,768]{1,0:T(8,128)} %get-tuple-element.7.grad, ...), custom_call_target="tpu_custom_call" | custom-call | tf_op jit(solution)/shard_map/hop/pallas_call | solution.py:353
  223.8 0.0 copy-start.1
  223.8 2.5 %convert_element_type.7 = bf16[512,768]{1,0:T(8,128)(2,1)} convert(f32[512,768]{1,0:T(8,128)} %get-tuple-element.8) | non-fusion elementwise | flops 393216 | bytes 2359296 | tf_op jit(solution)/shard_map/convert_element_type | solution.py:413
  226.3 0.0 copy-done.1
  226.3 0.0 copy-start
  226.3 1.4 copy.19
  227.7 1.1 copy-done
  228.8 1.4 copy.20
Async XLA Ops:
  2.0 16.5 %all-to-all-start = ((s32[32,1,1]{2,1,0:T(1,128)}), s32[32,1,1]{2,1,0:T(1,128)S(1)}, u32[]{:S(2)}, u32[]{:S(2)}) async-start(s32[32,1,1]{2,1,0:T(1,128)} %copy.15), calls=%async_computation | async-start | bytes 32768 | tf_op jit(solution)/shard_map/all_to_all | solution.py:407
  223.8 2.5 %copy-start.1 = (f32[768,768]{1,0:T(8,128)S(1)}, f32[768,768]{1,0:T(8,128)}, u32[]{:S(2)}) copy-start(f32[768,768]{1,0:T(8,128)} %get-tuple-element.15) | copy-start | bytes 7077892
  226.3 2.5 %copy-start = (f32[768,768]{1,0:T(8,128)S(1)}, f32[768,768]{1,0:T(8,128)}, u32[]{:S(2)}) copy-start(f32[768,768]{1,0:T(8,128)} %get-tuple-element.16) | copy-start | bytes 7077892

commit v2 on v1

v2 whole, which is shorter than its diff:
```python
import functools

import jax
import jax.numpy as jnp
from jax import lax
from jax.experimental import pallas as pl
from jax.experimental.pallas import tpu as pltpu
from jax.sharding import PartitionSpec as P

MESH = pl.DeviceIdType.MESH
SIDE = 4

STEP_US = {"arrive": 0.12, "sweep": 0.7, "late": 0.7, "grad": 1.0}
LINK_US = 2 * 0.1966 / 0.090
X_US = LINK_US
CORE_US = 0.1966 / 0.3
DELAY_US = 1.5
LATE_PARTS = 8
QUEUE_US = 6.0


def onward(dy, dz, b, part):
    first, second = (0, 1) if b == 0 else (1, 0)
    pos = (dy, dz)

    def step(axis, way):
        new = list(pos)
        new[axis] = (new[axis] + way) % SIDE
        return (new[0], new[1], b, part, axis, way)

    d1, d2 = pos[first], pos[second]
    moved = []
    if d2 == 0:
        if d1 == 0:
            moved += [step(first, 1), step(first, -1)]
        elif (d1, part) == (1, 0):
            moved.append(step(first, 1))
        elif (d1, part) == (3, 1):
            moved.append(step(first, -1))
        moved += [step(second, 1), step(second, -1)]
    elif (d2, part) == (1, 0):
        moved.append(step(second, 1))
    elif (d2, part) == (3, 1):
        moved.append(step(second, -1))
    return moved


def own_copies():
    first, rest = {0: [], 1: []}, []
    for b in range(2):
        for part in range(2):
            moved = onward(0, 0, b, part)
            first[b] += moved[:2]
            rest += moved[2:]
    order = lambda key: (key[3] if key[5] == 1 else 1 - key[3])
    return sorted(first[0], key=order), sorted(first[1], key=order), sorted(rest, key=order)


def plan():
    free = {}
    here = {}

    def send(link, key, cost, now):
        start = max(free.get(link, 0.0), now)
        free[link] = start + cost
        here[key] = start + cost + DELAY_US

    held = []

    def flush():
        nonlocal now
        for key in sorted(held, key=lambda key: key[0] != 0 and key[1] != 0):
            if free.get(key[4:], 0.0) <= now + QUEUE_US:
                held.remove(key)
                result.append(("send",) + key)
                send(key[4:], ("ring",) + key[:4], LINK_US, now)
                waiting.add(key[:4])

    def send_core(key, now):
        send("core", ("core",) + key, CORE_US, now)

    def send_peers(axis, name, cost, now):
        send((axis, 1), (name, 1), cost, now)
        send((axis, -1), (name, 3), cost, now)
        send((axis, 1), (name, 2), 2 * cost, now)

    result, waiting = [], set()
    now = 6.0
    first, second, rest = own_copies()
    for key in first + second:
        send(key[4:], ("ring",) + key[:4], LINK_US, 1.5)
        waiting.add(key[:4])
    held += rest
    for b in range(2):
        for part in range(2):
            send_core((0, 0, b, part), 3.0)
    send("core", ("pc", 0), 6 * CORE_US, 5.0)
    flush()
    seen = {(0, 0, b, part) for b in range(2) for part in range(2)}
    tasks = [("grad", n) for n in range(7)]
    tasks += [("sweep", 0, dy, dz) for dy in range(SIDE) for dz in range(SIDE) if (dy, dz) != (0, 0)]
    tasks += [("sweep", 1, dy, dz) for dy in range(SIDE) for dz in range(SIDE)]
    tasks += [("late", n) for n in range(LATE_PARTS)]
    needs = {0: ["pc"], 1: ["px"], 2: ["py"], 3: ["pz"], 4: ["ty"], 5: ["tx"], 6: ["tc"]}
    done_grad = -1

    def ready(task):
        if task[0] == "grad":
            if task[1] != done_grad + 1:
                return 1e9
            names = needs[task[1]]
            times = [here[key] for key in here if key[0] in names]
            return max(times)
        if task[0] == "late":
            times = [here[key] for key in here if key[0] == "member"]
            return max(times) if times else 1e9
        _, other, dy, dz = task
        keys = [(dy, dz, b, part) for b in range(2) for part in range(2)]
        if other == 0:
            return 0.0 if all(key in seen for key in keys) else 1e9
        return max(here.get(("core",) + key, 1e9) for key in keys)

    def price(task):
        if task[0] == "late":
            return STEP_US["late"] * 17 / LATE_PARTS
        return STEP_US[task[0]]

    def run(task):
        nonlocal now, done_grad
        now = max(now, ready(task)) + price(task)
        result.append(task)
        tasks.remove(task)
        if task[0] == "grad":
            done_grad = n = task[1]
            if n == 0:
                send_peers("x", "px", X_US * 0.75, now)
                send_peers("x", "member", 2 * X_US, now)
            elif n == 1:
                send_peers(0, "py", 0.375 * LINK_US, now)
            elif n == 2:
                send_peers(1, "pz", 0.375 * LINK_US, now)
            elif n == 3:
                send_peers(0, "ty", 0.375 * LINK_US, now)
            elif n == 4:
                send_peers("x", "tx", X_US * 0.75, now)
            elif n == 5:
                send("core", ("tc", 0), 3 * CORE_US, now)

    while waiting or held:
        flush()
        coming = min(waiting, key=lambda key: (here[("ring",) + key], key))
        arrival = here[("ring",) + coming]
        if arrival > now:
            able = [task for task in tasks if ready(task) <= now]
            able = [task for task in able if now + price(task) <= arrival + 0.5]
            if able:
                run(able[0])
                flush()
                continue
            soon = [task for task in tasks if task[0] == "grad" and ready(task) + 0.2 <= arrival]
            if soon:
                run(soon[0])
                flush()
                continue
        now = max(now, arrival) + STEP_US["arrive"]
        waiting.remove(coming)
        seen.add(coming)
        result.append(("arrive",) + coming)
        held += onward(*coming)
        flush()
        send_core(coming, now)
    while tasks:
        run(min(tasks, key=lambda task: (ready(task), task[0])))
    return result, now


def slope(value):
    sig = jax.nn.sigmoid(value)
    return sig * (1.0 + value * (1.0 - sig))


def across(left, right, dims):
    return lax.dot_general(left, right, (dims, ((), ())), preferred_element_type=jnp.float32)


def hop_kernel(scale, is_first, *refs):
    (slots, targets, count, lists, picks_in, agg, weight, grad, values_hbm), refs = refs[:9], refs[9:]
    out_ref, gout = refs[:2]
    refs = refs[2:]
    if is_first:
        picks_out, refs = refs[0], refs[1:]
    (
        pool, values, lhs, member_out, member_in, pull,
        part, part_core, part_x_out, part_x_in, part_y, part_y_in, part_z, total_y, total,
        values_sem, ring_send, ring_recv, core_send, core_recv, member_send, member_recv,
        pc_send, pc_recv, px_send, px_recv, py_send, py_recv, pz_send, pz_recv,
        ty_send, ty_recv, tx_send, tx_recv, tc_send, tc_recv,
    ), refs = refs[:36], refs[36:]
    if is_first:
        out = out_ref
        table, table_smem, picks_sem, kc_send, kc_recv, ky_send, ky_recv, kz_send, kz_recv = refs
        picks = picks_out
    else:
        (out,) = refs
        picks = picks_in
    blk = values.shape[1]
    width = weight.shape[0]
    slot_total = values.shape[0]
    half = blk // 2
    cut = min(256, width)
    m = lax.axis_index("member")
    g = lax.axis_index("group")
    y, z, c = g // (2 * SIDE), (g // 2) % SIDE, g % 2
    peers = range(1, SIDE)

    def at(dy, dz, other=0):
        core = c if other == 0 else 1 - c
        return (((y + dy) % SIDE) * SIDE + (z + dz) % SIDE) * 2 + core

    partner = {"group": at(0, 0, 1)}

    load_values = pltpu.make_async_copy(values_hbm, values, values_sem)
    load_values.start()

    barrier = pltpu.get_barrier_semaphore()
    for d in peers:
        for peer in ({"group": at(d, 0)}, {"group": at(0, d)}, {"member": (m + d) % SIDE}):
            pl.semaphore_signal(barrier, inc=1, device_id=peer, device_id_type=MESH)
    pl.semaphore_signal(barrier, inc=1, device_id=partner, device_id_type=MESH)

    def remote(src, dst, send, recv, peer):
        return pltpu.make_async_remote_copy(
            src_ref=src, dst_ref=dst, send_sem=send, recv_sem=recv, device_id=peer, device_id_type=MESH
        )

    sent = []

    def launch(copies):
        for copy in copies:
            copy.start()
            sent.append(copy)

    def ring(dy, dz, b, half_no, axis, way):
        rows = pl.ds(half_no * half, half)
        sdy, sdz = ((dy - way) % SIDE, dz) if axis == 0 else (dy, (dz - way) % SIDE)
        return remote(
            pool.at[0, sdy * SIDE + sdz, b, rows],
            pool.at[0, dy * SIDE + dz, b, rows],
            ring_send.at[dy * SIDE + dz, b, half_no],
            ring_recv.at[dy * SIDE + dz, b, half_no],
            {"group": at(way, 0) if axis == 0 else at(0, way)},
        )

    def wait_half(dy, dz, b, half_no):
        axis, d = (1, dz) if b == 0 else (0, dy)
        if d == 0:
            axis, d = (0, dy) if b == 0 else (1, dz)
        way = {1: 1, 3: -1, 2: 1 - 2 * half_no}[d]
        ring(dy, dz, b, half_no, axis, way).wait_recv()

    def to_core(dy, dz, b, half_no):
        rows = pl.ds(half_no * half, half)
        r = dy * SIDE + dz
        return remote(
            pool.at[0, r, b, rows], pool.at[1, r, b, rows],
            core_send.at[r, b, half_no], core_recv.at[r, b, half_no], partner,
        )

    if is_first:
        kc = remote(table.at[0, 0, 0], table.at[0, 0, 1], kc_send, kc_recv, partner)
        ky = [
            remote(table.at[0, 0], table.at[0, d], ky_send.at[d - 1], ky_recv.at[d - 1], {"group": at(d, 0)})
            for d in peers
        ]
        kz = [
            remote(table.at[0], table.at[d], kz_send.at[d - 1], kz_recv.at[d - 1], {"group": at(0, d)})
            for d in peers
        ]
        table[0, 0, 0] = jnp.broadcast_to(picks_in[...], table.shape[3:])

    rows_at = min(128, blk)
    own_first = own_copies()

    def own_block(b):
        @pl.loop(0, blk // rows_at)
        def _(i):
            inner = pl.ds(pl.multiple_of(i * rows_at, rows_at), rows_at)
            rows = pl.ds(pl.multiple_of(b * blk + i * rows_at, rows_at), rows_at)
            lift = across(agg[rows, :], weight[...], ((1,), (0,)))
            pulled = (grad[rows, :].astype(jnp.float32) * slope(lift)).astype(jnp.bfloat16)
            pull[rows, :] = pulled
            back = across(pulled, weight[...], ((1,), (1,))).astype(jnp.bfloat16)
            pool[0, 0, b, inner, :] = back

    pl.semaphore_wait(barrier, 3 * (SIDE - 1) + 1)
    if is_first:
        launch([kc])
    own_block(0)
    if is_first:
        kc.wait_recv()
        launch(ky)
    launch([ring(*key) for key in own_first[0]])
    own_block(1)
    if is_first:
        for copy in ky:
            copy.wait_recv()
        launch(kz)
    launch([ring(*key) for key in own_first[1]])
    order = plan()[0]
    while order[0][0] == "send":
        launch([ring(*order.pop(0)[1:])])
    launch([to_core(0, 0, b, part_no) for b in range(2) for part_no in range(2)])

    half_rows, x_rows = width // 2, width // 8
    y_rows = x_rows // SIDE

    @pl.loop(0, width // cut)
    def _(i):
        rows = pl.ds(pl.multiple_of(i * cut, cut), cut)
        part[rows, :] = across(agg[:, rows], pull[...], ((0,), (0,))) * scale

    mine = pl.ds(pl.multiple_of(c * half_rows, half_rows), half_rows)
    theirs = pl.ds(pl.multiple_of((1 - c) * half_rows, half_rows), half_rows)
    pc = remote(part.at[theirs], part_core, pc_send, pc_recv, partner)
    launch([pc])

    for d in peers:
        member_out[d - 1] = jnp.where(lists[(m + d) % SIDE] == 0, pool[0, 0, 0], pool[0, 0, 1])
    member_in[0] = pool[0, 0, 0]
    member_in[1] = pool[0, 0, 1]
    member_in[2 + m] = jnp.where(lists[m] == 0, pool[0, 0, 0], pool[0, 0, 1])
    out[...] = grad[...].astype(jnp.float32)
    load_values.wait()

    def member_copy(d, source):
        return remote(
            member_out.at[d - 1], member_in.at[2 + source], member_send.at[d - 1], member_recv.at[d - 1],
            {"member": (m + d) % SIDE},
        )

    def set_lhs(k, live):
        value = values[k].T
        zero = jnp.zeros_like(value)
        where = targets[k]
        lhs[0:blk, :] = jnp.where(jnp.logical_and(live, where == 0), value, zero)
        lhs[blk:2 * blk, :] = jnp.where(jnp.logical_and(live, where == 1), value, zero)

    def take_picks():
        for copy in kz:
            copy.wait_recv()
        fetch = pltpu.make_async_copy(table, table_smem, picks_sem)
        fetch.start()
        fetch.wait()
        for other in range(2):
            for dy in range(SIDE):
                for dz in range(SIDE):
                    picks_out[other * SIDE * SIDE + dy * SIDE + dz] = table_smem[dz, dy, other, 0, g]

    picks_here = [not is_first]

    def sweep(other, dy, dz):
        if not picks_here[0]:
            take_picks()
            picks_here[0] = True
        if other == 1:
            for b in range(2):
                for part_no in range(2):
                    to_core(dy, dz, b, part_no).wait_recv()
        groups = 2 * SIDE * SIDE
        r = dy * SIDE + dz
        set_lhs((at(-dy, -dz, other) - g - 1 + groups) % groups, True)
        pick = picks[other * SIDE * SIDE + r]

        for n in range(width // cut):
            cols = pl.ds(n * cut, cut)
            block = jnp.where(pick == 0, pool[other, r, 0, :, cols], pool[other, r, 1, :, cols])
            out[:, cols] += across(lhs[...], block, ((1,), (0,)))

    def late(number):
        start = 2 * SIDE * SIDE - 1
        total_late = slot_total - start
        if number == 0:
            for d in peers:
                member_copy(d, (m - d + SIDE) % SIDE).wait_recv()

        @pl.loop(start + total_late * number // LATE_PARTS, start + total_late * (number + 1) // LATE_PARTS)
        def _(k):
            set_lhs(k, k < count[0])

            for n in range(width // cut):
                cols = pl.ds(n * cut, cut)
                out[:, cols] += across(lhs[...], member_in[slots[k], :, cols], ((1,), (0,)))

    def px_copy(d):
        rows = pl.ds(pl.multiple_of(((m + d) % SIDE) * x_rows, x_rows), x_rows)
        return remote(
            part_x_out.at[rows], part_x_in.at[d - 1], px_send.at[d - 1], px_recv.at[d - 1],
            {"member": (m + d) % SIDE},
        )

    def py_copy(d):
        rows = pl.ds(pl.multiple_of(((y + d) % SIDE) * y_rows, y_rows), y_rows)
        return remote(
            part_y.at[rows], part_y_in.at[d - 1], py_send.at[d - 1], py_recv.at[d - 1],
            {"group": at(d, 0)},
        )

    def pz_copy(d, place):
        return remote(
            part_z.at[z], part_z.at[place], pz_send.at[d - 1], pz_recv.at[d - 1], {"group": at(0, d)}
        )

    def ty_copy(d, place):
        rows = pl.ds(pl.multiple_of(y * y_rows, y_rows), y_rows)
        there = pl.ds(pl.multiple_of(place * y_rows, y_rows), y_rows)
        return remote(
            total_y.at[rows], total_y.at[there], ty_send.at[d - 1], ty_recv.at[d - 1], {"group": at(d, 0)}
        )

    def tx_copy(d, place):
        rows = pl.ds(pl.multiple_of(c * half_rows + m * x_rows, x_rows), x_rows)
        there = pl.ds(pl.multiple_of(c * half_rows + place * x_rows, x_rows), x_rows)
        return remote(
            total.at[rows], total.at[there], tx_send.at[d - 1], tx_recv.at[d - 1],
            {"member": (m + d) % SIDE},
        )

    def tc_copy(there):
        return remote(total.at[mine], total.at[there], tc_send, tc_recv, partner)

    x_mine = pl.ds(pl.multiple_of(c * half_rows + m * x_rows, x_rows), x_rows)
    y_mine = pl.ds(pl.multiple_of(y * y_rows, y_rows), y_rows)

    def grad_step(number):
        if number == 0:
            pc.wait_recv()
            part[mine, :] += part_core[...]
            part_x_out[...] = part[mine, :].astype(jnp.bfloat16)
            launch([px_copy(d) for d in peers])
            launch([member_copy(d, m) for d in peers])
        elif number == 1:
            for d in peers:
                px_copy(d).wait_recv()
            summed = part[x_mine, :]
            for d in peers:
                summed += part_x_in[d - 1].astype(jnp.float32)
            part_y[...] = summed
            launch([py_copy(d) for d in peers])
        elif number == 2:
            for d in peers:
                py_copy(d).wait_recv()
            summed = part_y[y_mine, :]
            for d in peers:
                summed += part_y_in[d - 1]
            part_z[z] = summed
            launch([pz_copy(d, z) for d in peers])
        elif number == 3:
            for d in peers:
                pz_copy(d, (z - d + SIDE) % SIDE).wait_recv()
            total_y[y_mine, :] = (part_z[0] + part_z[1]) + (part_z[2] + part_z[3])
            launch([ty_copy(d, y) for d in peers])
        elif number == 4:
            for d in peers:
                ty_copy(d, (y - d + SIDE) % SIDE).wait_recv()
            total[x_mine, :] = total_y[...].astype(jnp.bfloat16)
            launch([tx_copy(d, m) for d in peers])
        elif number == 5:
            for d in peers:
                tx_copy(d, (m - d + SIDE) % SIDE).wait_recv()
            launch([tc_copy(mine)])
        elif number == 6:
            tc_copy(theirs).wait_recv()
            gout[...] = total[...].astype(jnp.float32)

    for task in order:
        if task[0] == "arrive":
            wait_half(*task[1:])
            launch([to_core(*task[1:])])
        elif task[0] == "send":
            launch([ring(*task[1:])])
        elif task[0] == "sweep":
            sweep(*task[1:])
        elif task[0] == "late":
            late(task[1])
        else:
            grad_step(task[1])

    if not is_first:
        out_ref[...] = out[...].astype(out_ref.dtype)
    for copy in sent:
        copy.wait_send()


def hop(is_first, slots, targets, count, lists, picks, agg, weight, grad, values, scale):
    rows, width = agg.shape
    slot_total, blk, _ = values.shape
    bf16, f32, i32 = jnp.bfloat16, jnp.float32, jnp.int32
    half_rows, x_rows = width // 2, width // 8
    y_rows = x_rows // SIDE
    vmem, smem = pl.BlockSpec(memory_space=pltpu.VMEM), pl.BlockSpec(memory_space=pltpu.SMEM)
    dma = pltpu.SemaphoreType.DMA
    peers = dma((SIDE - 1,))
    out_shape = [
        jax.ShapeDtypeStruct((rows, width), f32 if is_first else bf16),
        jax.ShapeDtypeStruct((width, width), f32),
    ]
    out_specs = [vmem, vmem]
    scratch = [
        pltpu.VMEM((2, SIDE * SIDE, 2, blk, width), bf16),
        pltpu.VMEM((slot_total, blk, blk), bf16),
        pltpu.VMEM((2 * blk, blk), bf16),
        pltpu.VMEM((SIDE - 1, blk, width), bf16),
        pltpu.VMEM((2 + SIDE, blk, width), bf16),
        pltpu.VMEM((rows, width), bf16),
        pltpu.VMEM((width, width), f32),
        pltpu.VMEM((half_rows, width), f32),
        pltpu.VMEM((half_rows, width), bf16),
        pltpu.VMEM((SIDE - 1, x_rows, width), bf16),
        pltpu.VMEM((x_rows, width), f32),
        pltpu.VMEM((SIDE - 1, y_rows, width), f32),
        pltpu.VMEM((SIDE, y_rows, width), f32),
        pltpu.VMEM((x_rows, width), f32),
        pltpu.VMEM((width, width), bf16),
        dma(()),
        dma((SIDE * SIDE, 2, 2)), dma((SIDE * SIDE, 2, 2)),
        dma((SIDE * SIDE, 2, 2)), dma((SIDE * SIDE, 2, 2)),
        peers, peers, dma(()), dma(()),
        peers, peers, peers, peers, peers, peers, peers, peers, peers, peers, dma(()), dma(()),
    ]
    if is_first:
        out_shape.append(jax.ShapeDtypeStruct((2 * SIDE * SIDE,), i32))
        out_specs.append(smem)
        scratch += [
            pltpu.VMEM((SIDE, SIDE, 2, 8, 128), i32),
            pltpu.SMEM((SIDE, SIDE, 2, 8, 128), i32),
            dma(()), dma(()), dma(()), peers, peers, peers, peers,
        ]
    else:
        scratch.append(pltpu.VMEM((rows, width), f32))
    return pl.pallas_call(
        functools.partial(hop_kernel, scale, is_first),
        out_shape=tuple(out_shape),
        in_specs=[smem] * 4 + [vmem if is_first else smem] + [vmem] * 3 + [pl.BlockSpec(memory_space=pl.ANY)],
        out_specs=tuple(out_specs),
        scratch_shapes=scratch,
        compiler_params=pltpu.CompilerParams(
            collective_id=0 if is_first else 1, has_side_effects=True, vmem_limit_bytes=60 << 20
        ),
        name="hop_two" if is_first else "hop_one",
    )(slots, targets, count, lists, picks, agg, weight, grad, values)


def body(
    agg_one,
    agg_two,
    grad_out,
    hop_one_weight,
    hop_two_weight,
    block_values,
    src_slot,
    dst_block,
    block_count,
    send_member,
    send_group,
):
    total_labels = agg_one.shape[0] * lax.axis_size("member") * lax.axis_size("group")
    scale = float(total_labels) ** (-0.5)
    graph = (src_slot[0], dst_block[0], block_count, send_member[0, :, 0])
    listed = jnp.pad(send_group, ((0, 0), (0, 128 - send_group.shape[1])))
    carry, grad_w_two, picks = hop(
        True, *graph, listed, agg_two, hop_two_weight, grad_out, block_values, scale
    )
    emb, grad_w_one = hop(
        False, *graph, picks, agg_one, hop_one_weight, carry, block_values, scale
    )
    return (emb, grad_w_one, grad_w_two)


def solution(mesh):
    in_specs = (
        P(("member", "group"), None),
        P(("member", "group"), None),
        P(("member", "group"), None),
        P(),
        P(),
        P(("member", "group"), None, None),
        P(("member", "group"), None),
        P(("member", "group"), None),
        P(("member", "group")),
        P(("member", "group"), None, None),
        P(("member", "group"), None),
    )
    out_specs = (P(("member", "group"), None), P(), P())
    return jax.shard_map(body, mesh=mesh, in_specs=in_specs, out_specs=out_specs, check_vma=False)
```

time: 231 us -> 193 us (0.84)
  Pallas kernels: 204 us -> 183 us
  starting transfers between devices: 9.6 us -> 0 us
  other arithmetic: 6.08 us -> 0 us
  waiting for transfers between devices: 3.83 us -> 0 us
  local copies, waits for them, and re-layouts: 5.27 us -> 8.01 us
    pallas_call x2, Pallas kernels: 204 us -> 183 us  [hop(): pl.pallas_call(functools.partial(hop_kernel, scale, is_first), out_shape=...]
    all_to_all x1 -> x0, starting transfers between devices: 9.6 us -> none  [body(): lax.all_to_all(send_group[0], 'group', split_axis=0, concat_axis=0, tiled...]
    convert_element_type x2 -> x0, other arithmetic: 4.9 us -> none  [the longest x1 2.52 us: body(): return (emb.astype(jnp.bfloat16), grad_w_one, grad_w_two)]
    all_to_all x1 -> x0, waiting for transfers between devices: 3.83 us -> none  [body(): lax.all_to_all(send_group[0], 'group', split_axis=0, concat_axis=0, tiled...]
    unnamed x6 -> x5, local copies, waits for them, and re-layouts: 3.93 us -> 6.84 us
  transfers between devices with their start and end apart: 1 -> 0, of which waited for: 1 -> 0; matrix products, arithmetic and copies ran while one was open for 1% -> 0% of each run, Pallas kernels for 0% -> 0%
where the time goes in v2:
time: 193 us
  Pallas kernels  183 us (95%)
  local copies, waits for them, and re-layouts  8.01 us (4%)
    pallas_call x2, Pallas kernels, hop(): pl.pallas_call(functools.partial(hop_kernel, scale, is_first), out_shape=...  183 us
    unnamed x5, local copies, waits for them, and re-layouts  6.84 us

profile of v2, /device:TPU:1, one launch (start us, length us, event | category | flops | bytes accessed | tf_op | source)
XLA Modules:
  0.0 192.7 jit_solution(6541356674896714182)
XLA Ops:
  1.3 1.2 pad.4.refs_4_
  2.4 95.5 %hop_two.1 = (f32[512,768]{1,0:T(8,128)}, f32[768,768]{1,0:T(8,128)}, s32[32]{0:T(128)}) custom-call(s32[48]{0:T(128)} %bitcast.3, s32[48]{0:T(128)} %bitcast.5, s32[1]{0:T(128)S(6)} %copy.17.refs_2_, s32[4]{0:T(128)} %bitcast.7, s32[1,128]{1,0:T(1,128)} %pad.4.refs_4_, bf16[512,768]{1,0:T(8,128)(2,1)} %refs_5_.2, bf16[768,768]{1,0:T(8,128)(2,1)} %refs_6_.2, ...), custom_call_target="tpu_custom_call" | custom-call | tf_op jit(solution)/shard_map/hop_two/pallas_call | solution.py:540
  98.0 87.9 %hop_one.1 = (bf16[512,768]{1,0:T(8,128)(2,1)}, f32[768,768]{1,0:T(8,128)}) custom-call(s32[48]{0:T(128)} %bitcast.4, s32[48]{0:T(128)} %bitcast.6, s32[1]{0:T(128)S(6)} %copy.17.refs_2_, s32[4]{0:T(128)} %bitcast.8, s32[32]{0:T(128)} %get-tuple-element.8.refs_4_, bf16[512,768]{1,0:T(8,128)(2,1)} %refs_5_.3, bf16[768,768]{1,0:T(8,128)(2,1)} %refs_6_.3, ...), custom_call_target="tpu_custom_call" | custom-call | tf_op jit(solution)/shard_map/hop_one/pallas_call | solution.py:540
  185.8 2.1 %copy.18 = bf16[512,768]{1,0:T(8,128)(2,1)} copy(bf16[512,768]{1,0:T(8,128)(2,1)} %get-tuple-element.16) | data formatting | bytes 1572864
  187.9 0.0 copy-start
  187.9 3.4 %copy.19 = f32[768,768]{1,0:T(8,128)} copy(f32[768,768]{1,0:T(8,128)} %get-tuple-element.17) | data formatting | bytes 4718592
  191.3 0.0 copy-done
  191.3 1.4 copy.20
Async XLA Ops:
  187.9 3.4 %copy-start = (f32[768,768]{1,0:T(8,128)S(1)}, f32[768,768]{1,0:T(8,128)}, u32[]{:S(2)}) copy-start(f32[768,768]{1,0:T(8,128)} %get-tuple-element.18) | copy-start | bytes 7077892

commit v3 on v2

--- a/solution.py
+++ b/solution.py
@@ -16,7 +16,7 @@
 CORE_US = 0.1966 / 0.3
 DELAY_US = 1.5
 LATE_PARTS = 8
-QUEUE_US = 6.0
+QUEUE_US = 4.0
 
 
 def onward(dy, dz, b, part):
@@ -46,14 +46,17 @@
 
 
 def own_copies():
-    first, rest = {0: [], 1: []}, []
-    for b in range(2):
-        for part in range(2):
-            moved = onward(0, 0, b, part)
-            first[b] += moved[:2]
-            rest += moved[2:]
-    order = lambda key: (key[3] if key[5] == 1 else 1 - key[3])
-    return sorted(first[0], key=order), sorted(first[1], key=order), sorted(rest, key=order)
+    early = [
+        [(1, 0, 0, 0, 0, 1), (0, 1, 0, 0, 1, 1)],
+        [(3, 0, 0, 1, 0, -1), (0, 3, 0, 1, 1, -1), (1, 0, 0, 1, 0, 1), (3, 0, 0, 0, 0, -1)],
+        [(0, 1, 1, 0, 1, 1)],
+        [(0, 3, 1, 1, 1, -1), (0, 1, 1, 1, 1, 1), (0, 3, 1, 0, 1, -1)],
+    ]
+    rest = [key for b in range(2) for part in range(2) for key in onward(0, 0, b, part)]
+    for group in early:
+        for key in group:
+            rest.remove(key)
+    return early, sorted(rest, key=lambda key: key[3] if key[5] == 1 else 1 - key[3])
 
 
 def plan():
@@ -86,10 +89,11 @@
 
     result, waiting = [], set()
     now = 6.0
-    first, second, rest = own_copies()
-    for key in first + second:
-        send(key[4:], ("ring",) + key[:4], LINK_US, 1.5)
-        waiting.add(key[:4])
+    early, rest = own_copies()
+    for number, group in enumerate(early):
+        for key in group:
+            send(key[4:], ("ring",) + key[:4], LINK_US, 1.5 + number)
+            waiting.add(key[:4])
     held += rest
     for b in range(2):
         for part in range(2):
@@ -136,11 +140,11 @@
                 send_peers("x", "px", X_US * 0.75, now)
                 send_peers("x", "member", 2 * X_US, now)
             elif n == 1:
-                send_peers(0, "py", 0.375 * LINK_US, now)
+                send_peers(0, "py", 0.1875 * LINK_US, now)
             elif n == 2:
-                send_peers(1, "pz", 0.375 * LINK_US, now)
+                send_peers(1, "pz", 0.1875 * LINK_US, now)
             elif n == 3:
-                send_peers(0, "ty", 0.375 * LINK_US, now)
+                send_peers(0, "ty", 0.1875 * LINK_US, now)
             elif n == 4:
                 send_peers("x", "tx", X_US * 0.75, now)
             elif n == 5:
@@ -185,17 +189,17 @@
 
 def hop_kernel(scale, is_first, *refs):
     (slots, targets, count, lists, picks_in, agg, weight, grad, values_hbm), refs = refs[:9], refs[9:]
-    out_ref, gout = refs[:2]
+    out_ref, total = refs[:2]
     refs = refs[2:]
     if is_first:
         picks_out, refs = refs[0], refs[1:]
     (
         pool, values, lhs, member_out, member_in, pull,
-        part, part_core, part_x_out, part_x_in, part_y, part_y_in, part_z, total_y, total,
+        part, part_core, part_x_out, part_x_in, part_y, part_y_in, part_z, total_y,
         values_sem, ring_send, ring_recv, core_send, core_recv, member_send, member_recv,
         pc_send, pc_recv, px_send, px_recv, py_send, py_recv, pz_send, pz_recv,
         ty_send, ty_recv, tx_send, tx_recv, tc_send, tc_recv,
-    ), refs = refs[:36], refs[36:]
+    ), refs = refs[:35], refs[35:]
     if is_first:
         out = out_ref
         table, table_smem, picks_sem, kc_send, kc_recv, ky_send, ky_recv, kz_send, kz_recv = refs
@@ -276,43 +280,42 @@
             remote(table.at[0], table.at[d], kz_send.at[d - 1], kz_recv.at[d - 1], {"group": at(0, d)})
             for d in peers
         ]
-        table[0, 0, 0] = jnp.broadcast_to(picks_in[...], table.shape[3:])
-
-    rows_at = min(128, blk)
-    own_first = own_copies()
-
-    def own_block(b):
-        @pl.loop(0, blk // rows_at)
-        def _(i):
-            inner = pl.ds(pl.multiple_of(i * rows_at, rows_at), rows_at)
-            rows = pl.ds(pl.multiple_of(b * blk + i * rows_at, rows_at), rows_at)
-            lift = across(agg[rows, :], weight[...], ((1,), (0,)))
-            pulled = (grad[rows, :].astype(jnp.float32) * slope(lift)).astype(jnp.bfloat16)
-            pull[rows, :] = pulled
-            back = across(pulled, weight[...], ((1,), (1,))).astype(jnp.bfloat16)
-            pool[0, 0, b, inner, :] = back
+        table[0, 0, 0] = jnp.zeros(table.shape[3:], jnp.int32)
+        table[0, 0, 0, 0:1, 0:picks_in.shape[1]] = picks_in[...]
+
+    early = own_copies()[0]
+
+    def own_part(b, part_no):
+        rows = pl.ds(b * blk + part_no * half, half)
+        lift = across(agg[rows, :], weight[...], ((1,), (0,)))
+        pulled = (grad[rows, :].astype(jnp.float32) * slope(lift)).astype(jnp.bfloat16)
+        pull[rows, :] = pulled
+        back = across(pulled, weight[...], ((1,), (1,))).astype(jnp.bfloat16)
+        pool[0, 0, b, pl.ds(part_no * half, half), :] = back
+        launch([ring(*key) for key in early[b * 2 + part_no]])
 
     pl.semaphore_wait(barrier, 3 * (SIDE - 1) + 1)
     if is_first:
         launch([kc])
-    own_block(0)
+    own_part(0, 0)
     if is_first:
         kc.wait_recv()
         launch(ky)
-    launch([ring(*key) for key in own_first[0]])
-    own_block(1)
+    own_part(0, 1)
+    own_part(1, 0)
     if is_first:
         for copy in ky:
             copy.wait_recv()
         launch(kz)
-    launch([ring(*key) for key in own_first[1]])
+    own_part(1, 1)
     order = plan()[0]
     while order[0][0] == "send":
         launch([ring(*order.pop(0)[1:])])
     launch([to_core(0, 0, b, part_no) for b in range(2) for part_no in range(2)])
 
     half_rows, x_rows = width // 2, width // 8
-    y_rows = x_rows // SIDE
+    lanes = width // 128
+    y_rows = x_rows * lanes // SIDE
 
     @pl.loop(0, width // cut)
     def _(i):
@@ -348,7 +351,7 @@
     def take_picks():
         for copy in kz:
             copy.wait_recv()
-        fetch = pltpu.make_async_copy(table, table_smem, picks_sem)
+        fetch = pltpu.make_async_copy(table.at[:, :, :, pl.ds(0, 1)], table_smem, picks_sem)
         fetch.start()
         fetch.wait()
         for other in range(2):
@@ -444,25 +447,28 @@
             summed = part[x_mine, :]
             for d in peers:
                 summed += part_x_in[d - 1].astype(jnp.float32)
-            part_y[...] = summed
+            for j in range(lanes):
+                part_y[j * x_rows:(j + 1) * x_rows, :] = summed[:, j * 128:(j + 1) * 128].astype(jnp.bfloat16)
             launch([py_copy(d) for d in peers])
         elif number == 2:
             for d in peers:
                 py_copy(d).wait_recv()
-            summed = part_y[y_mine, :]
-            for d in peers:
-                summed += part_y_in[d - 1]
-            part_z[z] = summed
+            summed = part_y[y_mine, :].astype(jnp.float32)
+            for d in peers:
+                summed += part_y_in[d - 1].astype(jnp.float32)
+            part_z[z] = summed.astype(jnp.bfloat16)
             launch([pz_copy(d, z) for d in peers])
         elif number == 3:
             for d in peers:
                 pz_copy(d, (z - d + SIDE) % SIDE).wait_recv()
-            total_y[y_mine, :] = (part_z[0] + part_z[1]) + (part_z[2] + part_z[3])
+            four = [part_z[n].astype(jnp.float32) for n in range(SIDE)]
+            total_y[y_mine, :] = ((four[0] + four[1]) + (four[2] + four[3])).astype(jnp.bfloat16)
             launch([ty_copy(d, y) for d in peers])
         elif number == 4:
             for d in peers:
                 ty_copy(d, (y - d + SIDE) % SIDE).wait_recv()
-            total[x_mine, :] = total_y[...].astype(jnp.bfloat16)
+            for j in range(lanes):
+                total[x_mine, j * 128:(j + 1) * 128] = total_y[j * x_rows:(j + 1) * x_rows, :]
             launch([tx_copy(d, m) for d in peers])
         elif number == 5:
             for d in peers:
@@ -470,7 +476,6 @@
             launch([tc_copy(mine)])
         elif number == 6:
             tc_copy(theirs).wait_recv()
-            gout[...] = total[...].astype(jnp.float32)
 
     for task in order:
         if task[0] == "arrive":
@@ -496,13 +501,14 @@
     slot_total, blk, _ = values.shape
     bf16, f32, i32 = jnp.bfloat16, jnp.float32, jnp.int32
     half_rows, x_rows = width // 2, width // 8
-    y_rows = x_rows // SIDE
+    lanes = width // 128
+    y_rows = x_rows * lanes // SIDE
     vmem, smem = pl.BlockSpec(memory_space=pltpu.VMEM), pl.BlockSpec(memory_space=pltpu.SMEM)
     dma = pltpu.SemaphoreType.DMA
     peers = dma((SIDE - 1,))
     out_shape = [
         jax.ShapeDtypeStruct((rows, width), f32 if is_first else bf16),
-        jax.ShapeDtypeStruct((width, width), f32),
+        jax.ShapeDtypeStruct((width, width), bf16),
     ]
     out_specs = [vmem, vmem]
     scratch = [
@@ -516,11 +522,10 @@
         pltpu.VMEM((half_rows, width), f32),
         pltpu.VMEM((half_rows, width), bf16),
         pltpu.VMEM((SIDE - 1, x_rows, width), bf16),
-        pltpu.VMEM((x_rows, width), f32),
-        pltpu.VMEM((SIDE - 1, y_rows, width), f32),
-        pltpu.VMEM((SIDE, y_rows, width), f32),
-        pltpu.VMEM((x_rows, width), f32),
-        pltpu.VMEM((width, width), bf16),
+        pltpu.VMEM((x_rows * lanes, 128), bf16),
+        pltpu.VMEM((SIDE - 1, y_rows, 128), bf16),
+        pltpu.VMEM((SIDE, y_rows, 128), bf16),
+        pltpu.VMEM((x_rows * lanes, 128), bf16),
         dma(()),
         dma((SIDE * SIDE, 2, 2)), dma((SIDE * SIDE, 2, 2)),
         dma((SIDE * SIDE, 2, 2)), dma((SIDE * SIDE, 2, 2)),
@@ -532,7 +537,7 @@
         out_specs.append(smem)
         scratch += [
             pltpu.VMEM((SIDE, SIDE, 2, 8, 128), i32),
-            pltpu.SMEM((SIDE, SIDE, 2, 8, 128), i32),
+            pltpu.SMEM((SIDE, SIDE, 2, 1, 128), i32),
             dma(()), dma(()), dma(()), peers, peers, peers, peers,
         ]
     else:
@@ -566,14 +571,13 @@
     total_labels = agg_one.shape[0] * lax.axis_size("member") * lax.axis_size("group")
     scale = float(total_labels) ** (-0.5)
     graph = (src_slot[0], dst_block[0], block_count, send_member[0, :, 0])
-    listed = jnp.pad(send_group, ((0, 0), (0, 128 - send_group.shape[1])))
     carry, grad_w_two, picks = hop(
-        True, *graph, listed, agg_two, hop_two_weight, grad_out, block_values, scale
+        True, *graph, send_group, agg_two, hop_two_weight, grad_out, block_values, scale
     )
     emb, grad_w_one = hop(
         False, *graph, picks, agg_one, hop_one_weight, carry, block_values, scale
     )
-    return (emb, grad_w_one, grad_w_two)
+    return (emb, grad_w_one.astype(jnp.float32), grad_w_two.astype(jnp.float32))
 
 
 def solution(mesh):

time: 193 us -> 176 us (0.912)
  Pallas kernels: 183 us -> 169 us
  local copies, waits for them, and re-layouts: 8.01 us -> 0.89 us
  other arithmetic: 0 us -> 4.52 us
    pallas_call x2, Pallas kernels: 183 us -> 169 us  [hop(): pl.pallas_call(functools.partial(hop_kernel, scale, is_first), out_shape=...]
    unnamed x5, local copies, waits for them, and re-layouts: 6.84 us -> 0.89 us
    convert_element_type x0 -> x2, other arithmetic: none -> 4.52 us  [body(): return (emb, grad_w_one.astype(jnp.float32), grad_w_two.astype(jnp.float32))]
where the time goes in v3:
time: 176 us; the launch traced here: 175 us
  Pallas kernels  169 us (96%)
  other arithmetic  4.52 us (3%)
    pallas_call x2, Pallas kernels, hop(): pl.pallas_call(functools.partial(hop_kernel, scale, is_first), out_shape=...  169 us
    convert_element_type x2, other arithmetic, body(): return (emb, grad_w_one.astype(jnp.float32), grad_w_two.astype(jnp.float32))  4.52 us

profile of v3, /device:TPU:1, one launch (start us, length us, event | category | flops | bytes accessed | tf_op | source)
XLA Modules:
  0.0 175.5 jit_solution(15592912506594204899)
XLA Ops:
  1.3 87.2 %hop_two.1 = (f32[512,768]{1,0:T(8,128)}, bf16[768,768]{1,0:T(8,128)(2,1)}, s32[32]{0:T(128)}) custom-call(s32[48]{0:T(128)} %bitcast.3, s32[48]{0:T(128)} %bitcast.5, s32[1]{0:T(128)S(6)} %copy.15.refs_2_, s32[4]{0:T(128)} %bitcast.7, s32[1,32]{1,0:T(1,128)} %refs_4_.1, bf16[512,768]{1,0:T(8,128)(2,1)} %refs_5_.2, bf16[768,768]{1,0:T(8,128)(2,1)} %refs_6_.2, ...), custom_call_target="tpu_custom_call" | custom-call | tf_op jit(solution)/shard_map/hop_two/pallas_call | solution.py:545
  88.5 81.6 %hop_one.1 = (bf16[512,768]{1,0:T(8,128)(2,1)}, bf16[768,768]{1,0:T(8,128)(2,1)}) custom-call(s32[48]{0:T(128)} %bitcast.4, s32[48]{0:T(128)} %bitcast.6, s32[1]{0:T(128)S(6)} %copy.15.refs_2_, s32[4]{0:T(128)} %bitcast.8, s32[32]{0:T(128)} %get-tuple-element.8.refs_4_, bf16[512,768]{1,0:T(8,128)(2,1)} %refs_5_.3, bf16[768,768]{1,0:T(8,128)(2,1)} %refs_6_.3, ...), custom_call_target="tpu_custom_call" | custom-call | tf_op jit(solution)/shard_map/hop_one/pallas_call | solution.py:545
  170.1 0.0 copy-start
  170.1 2.9 %convert_element_type.6 = f32[768,768]{1,0:T(8,128)} convert(bf16[768,768]{1,0:T(8,128)(2,1)} %get-tuple-element.11) | non-fusion elementwise | flops 589824 | bytes 3538944 | tf_op jit(solution)/shard_map/convert_element_type | solution.py:580
  173.0 0.0 copy-done
  173.0 0.0 copy-start.1
  173.0 1.6 convert_element_type.7
  174.6 0.0 copy-done.1
  174.6 0.9 copy.16
Async XLA Ops:
  170.1 3.0 %copy-start = (bf16[768,768]{1,0:T(8,128)(2,1)S(1)}, bf16[768,768]{1,0:T(8,128)(2,1)}, u32[]{:S(2)}) copy-start(bf16[768,768]{1,0:T(8,128)(2,1)} %get-tuple-element.12) | copy-start | bytes 3538948
  173.0 1.6 copy-start.1

commit v4 on v3

--- a/solution.py
+++ b/solution.py
@@ -16,7 +16,7 @@
 CORE_US = 0.1966 / 0.3
 DELAY_US = 1.5
 LATE_PARTS = 8
-QUEUE_US = 4.0
+QUEUE_US = 4.8
 
 
 def onward(dy, dz, b, part):
@@ -555,6 +555,29 @@
     )(slots, targets, count, lists, picks, agg, weight, grad, values)
 
 
+def finish_kernel(emb, one, two, emb_out, one_out, two_out):
+    emb_out[...] = emb[...]
+    one_out[...] = one[...].astype(jnp.float32)
+    two_out[...] = two[...].astype(jnp.float32)
+
+
+def finish(emb, one, two):
+    steps = 2
+    specs = [pl.BlockSpec((array.shape[0] // steps, array.shape[1]), lambda i: (i, 0)) for array in (emb, one, two)]
+    return pl.pallas_call(
+        finish_kernel,
+        grid=(steps,),
+        out_shape=(
+            jax.ShapeDtypeStruct(emb.shape, emb.dtype),
+            jax.ShapeDtypeStruct(one.shape, jnp.float32),
+            jax.ShapeDtypeStruct(two.shape, jnp.float32),
+        ),
+        in_specs=specs,
+        out_specs=tuple(specs),
+        name="finish",
+    )(emb, one, two)
+
+
 def body(
     agg_one,
     agg_two,
@@ -577,7 +600,7 @@
     emb, grad_w_one = hop(
         False, *graph, picks, agg_one, hop_one_weight, carry, block_values, scale
     )
-    return (emb, grad_w_one.astype(jnp.float32), grad_w_two.astype(jnp.float32))
+    return finish(emb, grad_w_one, grad_w_two)
 
 
 def solution(mesh):

time: 176 us -> 174 us (0.989)
  other arithmetic: 4.52 us -> 0 us
  Pallas kernels: 169 us -> 173 us
    convert_element_type x2 -> x0, other arithmetic: 4.52 us -> none  [body(): return (emb, grad_w_one.astype(jnp.float32), grad_w_two.astype(jnp.float32))]
    pallas_call x0 -> x1, Pallas kernels: none -> 3.97 us  [finish(): pl.pallas_call(finish_kernel, grid=(steps,), out_shape=(jax.ShapeDtypeStr...]
where the time goes in v4:
time: 174 us
  Pallas kernels  173 us (99%)
    pallas_call x2, Pallas kernels, hop(): pl.pallas_call(functools.partial(hop_kernel, scale, is_first), out_shape=...  169 us
    pallas_call x1, Pallas kernels, finish(): pl.pallas_call(finish_kernel, grid=(steps,), out_shape=(jax.ShapeDtypeStr...  3.97 us

profile of v4, /device:TPU:1, one launch (start us, length us, event | category | flops | bytes accessed | tf_op | source)
XLA Modules:
  0.0 174.1 jit_solution(15611755231779950900)
XLA Ops:
  1.3 87.4 %hop_two.1 = (f32[512,768]{1,0:T(8,128)}, bf16[768,768]{1,0:T(8,128)(2,1)}, s32[32]{0:T(128)}) custom-call(s32[48]{0:T(128)} %bitcast.3, s32[48]{0:T(128)} %bitcast.5, s32[1]{0:T(128)S(6)} %copy.14.refs_2_, s32[4]{0:T(128)} %bitcast.7, s32[1,32]{1,0:T(1,128)} %refs_4_.1, bf16[512,768]{1,0:T(8,128)(2,1)} %refs_5_.2, bf16[768,768]{1,0:T(8,128)(2,1)} %refs_6_.2, ...), custom_call_target="tpu_custom_call" | custom-call | tf_op jit(solution)/shard_map/hop_two/pallas_call | solution.py:545
  88.7 81.4 %hop_one.1 = (bf16[512,768]{1,0:T(8,128)(2,1)}, bf16[768,768]{1,0:T(8,128)(2,1)}) custom-call(s32[48]{0:T(128)} %bitcast.4, s32[48]{0:T(128)} %bitcast.6, s32[1]{0:T(128)S(6)} %copy.14.refs_2_, s32[4]{0:T(128)} %bitcast.8, s32[32]{0:T(128)} %get-tuple-element.8.refs_4_, bf16[512,768]{1,0:T(8,128)(2,1)} %refs_5_.3, bf16[768,768]{1,0:T(8,128)(2,1)} %refs_6_.3, ...), custom_call_target="tpu_custom_call" | custom-call | tf_op jit(solution)/shard_map/hop_one/pallas_call | solution.py:545
  170.1 4.0 %finish.1 = (bf16[512,768]{1,0:T(8,128)(2,1)}, f32[768,768]{1,0:T(8,128)}, f32[768,768]{1,0:T(8,128)}) custom-call(bf16[512,768]{1,0:T(8,128)(2,1)} %get-tuple-element.10.emb, bf16[768,768]{1,0:T(8,128)(2,1)} %get-tuple-element.11.one, bf16[768,768]{1,0:T(8,128)(2,1)} %get-tuple-element.12.two), custom_call_target="tpu_custom_call" | custom-call | tf_op jit(solution)/shard_map/finish/pallas_call | solution.py:567

commit v5 on v4

--- a/solution.py
+++ b/solution.py
@@ -156,7 +156,7 @@
         arrival = here[("ring",) + coming]
         if arrival > now:
             able = [task for task in tasks if ready(task) <= now]
-            able = [task for task in able if now + price(task) <= arrival + 0.5]
+            able = [task for task in able if now + price(task) <= arrival + 0.1]
             if able:
                 run(able[0])
                 flush()

time: 174 us -> 181 us (1.040)
  Pallas kernels: 173 us -> 179 us
    pallas_call x2, Pallas kernels: 169 us -> 175 us  [hop(): pl.pallas_call(functools.partial(hop_kernel, scale, is_first), out_shape=...]
where the time goes in v5:
time: 181 us
  Pallas kernels  179 us (99%)
    pallas_call x2, Pallas kernels, hop(): pl.pallas_call(functools.partial(hop_kernel, scale, is_first), out_shape=...  175 us
    pallas_call x1, Pallas kernels, finish(): pl.pallas_call(finish_kernel, grid=(steps,), out_shape=(jax.ShapeDtypeStr...  3.97 us

profile of v5, /device:TPU:1, one launch (start us, length us, event | category | flops | bytes accessed | tf_op | source)
XLA Modules:
  0.0 180.7 jit_solution(10536171503791290382)
XLA Ops:
  1.3 89.6 %hop_two.1 = (f32[512,768]{1,0:T(8,128)}, bf16[768,768]{1,0:T(8,128)(2,1)}, s32[32]{0:T(128)}) custom-call(s32[48]{0:T(128)} %bitcast.3, s32[48]{0:T(128)} %bitcast.5, s32[1]{0:T(128)S(6)} %copy.14.refs_2_, s32[4]{0:T(128)} %bitcast.7, s32[1,32]{1,0:T(1,128)} %refs_4_.1, bf16[512,768]{1,0:T(8,128)(2,1)} %refs_5_.2, bf16[768,768]{1,0:T(8,128)(2,1)} %refs_6_.2, ...), custom_call_target="tpu_custom_call" | custom-call | tf_op jit(solution)/shard_map/hop_two/pallas_call | solution.py:545
  90.9 85.8 %hop_one.1 = (bf16[512,768]{1,0:T(8,128)(2,1)}, bf16[768,768]{1,0:T(8,128)(2,1)}) custom-call(s32[48]{0:T(128)} %bitcast.4, s32[48]{0:T(128)} %bitcast.6, s32[1]{0:T(128)S(6)} %copy.14.refs_2_, s32[4]{0:T(128)} %bitcast.8, s32[32]{0:T(128)} %get-tuple-element.8.refs_4_, bf16[512,768]{1,0:T(8,128)(2,1)} %refs_5_.3, bf16[768,768]{1,0:T(8,128)(2,1)} %refs_6_.3, ...), custom_call_target="tpu_custom_call" | custom-call | tf_op jit(solution)/shard_map/hop_one/pallas_call | solution.py:545
  176.7 4.0 %finish.1 = (bf16[512,768]{1,0:T(8,128)(2,1)}, f32[768,768]{1,0:T(8,128)}, f32[768,768]{1,0:T(8,128)}) custom-call(bf16[512,768]{1,0:T(8,128)(2,1)} %get-tuple-element.10.emb, bf16[768,768]{1,0:T(8,128)(2,1)} %get-tuple-element.11.one, bf16[768,768]{1,0:T(8,128)(2,1)} %get-tuple-element.12.two), custom_call_target="tpu_custom_call" | custom-call | tf_op jit(solution)/shard_map/finish/pallas_call | solution.py:567
